TPU v7x, 32 devices: a whole 2x2x4 slice. The times are simulated.
32 devices in a mesh: pole: 4 (over y, x), row: 2 (over core), col: 4 (over z).
Axes of the slice: x: 2, y: 2, z: 4, core: 2. Of those that a mesh axis runs over, the one named last changes fastest.
Arguments:
- hamiltonian_panel: bfloat16 [6144, 512], P(('row', 'col'), 'pole'), may hold values from -0.005859375 to 0.005859375
- margin_panel: bfloat16 [6144, 512], P(('row', 'col'), 'pole'), may hold values from -0.0029296875 to 0.0029296875
- shifts: float32 [4, 2], P('pole'), may hold values from -2 to 2
- weights: float32 [4, 2], P('pole'), may hold values from 0.5 to 2
- pivot_inverse: float32 [4, 2, 512, 512], P('pole'), may hold values from -6 to 6
- selected_inverse: bfloat16 [4, 2, 6144, 6144], P('pole', None, 'row', 'col'), may hold values from -6 to 6
Outputs:
- inverse_column: float32 [4, 6144, 2, 512], P('pole', ('row', 'col'))
- inverse_pivot: float32 [4, 2, 512, 512], P('pole')
- density_column: float32 [6144, 512], P(('row', 'col'), 'pole')
- density_pivot: float32 [512, 512], P('pole')
All inputs are finite; a program needn't handle non-finite values.
Results may differ from a plain program's by a relative error of at most 0.0037.
Values may be sent and summed in bfloat16 or wider, within the bound.
A program may use at most 128 MiB of HBM per device.

v0:
```python
import jax
import jax.numpy as jnp
from jax import lax
from jax.sharding import PartitionSpec as P

PANEL = 512


def precise(left, right):
    return jnp.dot(left, right, precision=lax.Precision.HIGHEST, preferred_element_type=jnp.float32)


def factor_panel(hamiltonian, margin, shift, inverse):
    hamiltonian_f = hamiltonian.astype(jnp.float32)
    margin_f = margin.astype(jnp.float32)
    real_part = hamiltonian_f - shift[0] * margin_f
    imag_part = -shift[1] * margin_f
    lower_real = precise(real_part, inverse[0]) - precise(imag_part, inverse[1])
    lower_imag = precise(real_part, inverse[1]) + precise(imag_part, inverse[0])
    return jnp.stack([lower_real, lower_imag], axis=1).astype(jnp.bfloat16)


def apply_block(block_real, block_imag, lower):
    width = lower.shape[2]
    flat = lower.reshape(lower.shape[0], 2 * width)
    first = jnp.dot(block_real, flat, preferred_element_type=jnp.float32)
    second = jnp.dot(block_imag, flat, preferred_element_type=jnp.float32)
    return -jnp.stack(
        [first[:, :width] - second[:, width:], first[:, width:] + second[:, :width]], axis=1
    )


def pivot_term(lower, column):
    width = lower.shape[2]
    left = lower.astype(jnp.float32).reshape(lower.shape[0], 2 * width)
    right = column.reshape(column.shape[0], 2 * width)
    square = lax.dot_general(
        left,
        right,
        (((0,), (0,)), ((), ())),
        precision=lax.Precision.HIGHEST,
        preferred_element_type=jnp.float32,
    )
    return jnp.stack(
        [
            square[:width, :width] - square[width:, width:],
            square[:width, width:] + square[width:, :width],
        ]
    )


def body(hamiltonian_panel, margin_panel, shifts, weights, pivot_inverse, selected_inverse):
    shift = shifts[0]
    weight = weights[0]
    inverse = pivot_inverse[0]
    block = selected_inverse[0]
    span = block.shape[2]
    column_index = lax.axis_index("col")
    both = (
        lax.all_gather(hamiltonian_panel, "pole", axis=1, tiled=True),
        lax.all_gather(margin_panel, "pole", axis=1, tiled=True),
    )
    owned = factor_panel(both[0], both[1], shift, inverse)
    gathered = lax.all_gather(owned, ("row", "col"), axis=0, tiled=True)
    needed = lax.dynamic_slice_in_dim(gathered, column_index * span, span, 0)
    block_real = block[0]
    block_imag = block[1]
    column = lax.psum_scatter(
        apply_block(block_real, block_imag, needed), "col", scatter_dimension=0, tiled=True
    )
    pivot = inverse - lax.psum(pivot_term(owned, column), ("row", "col"))
    column_density = weight[0] * column[:, 0] - weight[1] * column[:, 1]
    pivot_density = weight[0] * pivot[0] - weight[1] * pivot[1]
    totals = lax.psum((column_density, pivot_density), "pole")
    portion = PANEL // lax.axis_size("pole")
    slot = lax.axis_index("pole")
    column_share = lax.dynamic_slice_in_dim(totals[0], slot * portion, portion, 1)
    pivot_share = lax.dynamic_slice_in_dim(totals[1], slot * portion, portion, 0)
    return (column[None], pivot[None], column_share, pivot_share)


def solution(mesh):
    return jax.shard_map(
        body,
        mesh=mesh,
        in_specs=(
            P(("row", "col"), "pole"),
            P(("row", "col"), "pole"),
            P("pole", None),
            P("pole", None),
            P("pole", None, None, None),
            P("pole", None, "row", "col"),
        ),
        out_specs=(
            P("pole", ("row", "col"), None, None),
            P("pole", None, None, None),
            P(("row", "col"), "pole"),
            P("pole", None),
        ),
        check_vma=False,
    )
```

profile of v0, /device:TPU:0, one launch (start us, length us, event | category | flops | bytes accessed | tf_op | source)
XLA Modules:
  0.0 594.3 jit_solution(16487910491604722457)
XLA Ops:
  7.2 0.0 all-gather.2.cloned.1.call-start
  7.2 13.8 %all_gather.10 = bf16[768,512]{1,0:T(8,128)(2,1)S(1)} all-gather(bf16[768,128]{1,0:T(8,128)(2,1)} %param.7), channel_id=1, replica_groups=mesh['pole'=4,'row'=2,'col'=4] {'pole'}, dimensions={1}, use_global_device_ids=true | all-gather | bytes 983040 | tf_op jit(solution)/shard_map/all_gather | solution.py:61
  21.0 1.3 fusion.42
  22.3 11.1 %all_gather.9 = bf16[768,512]{1,0:T(8,128)(2,1)S(1)} all-gather(bf16[768,128]{1,0:T(8,128)(2,1)} %param.6), channel_id=1, replica_groups=mesh['pole'=4,'row'=2,'col'=4] {'pole'}, dimensions={1}, use_global_device_ids=true | all-gather | bytes 983040 | tf_op jit(solution)/shard_map/all_gather | solution.py:60
  33.4 0.0 copy-start
  33.4 5.0 fusion.21
  38.4 0.0 copy-done
  38.4 3.7 fusion.19
  42.8 3.1 fusion.23
  45.8 3.1 fusion.24
  48.9 1.5 pad_maximum_fusion.1
  50.3 0.0 all-gather.2.cloned.1.call-update
  50.4 0.0 reduce-scatter.2.cloned.1.call-start
  50.4 117.1 %all-gather.2.cloned.1.call-done = bf16[6144,2,512]{0,2,1:T(8,128)(2,1)} async-done(((bf16[768,2,512]{0,2,1:T(8,128)(2,1)}), bf16[6144,2,512]{0,2,1:T(8,128)(2,1)}) %all-gather.2.cloned.1.call-update) | async-done | bytes 12582928 | tf_op jit(solution)/shard_map/all_gather | solution.py:64
  167.5 2.1 constant_dynamic-slice_fusion.2
  169.6 12.5 %fusion.6 = f32[3072,1024]{0,1:T(8,128)S(1)} fusion(bf16[1536,1024]{0,1:T(8,128)(2,1)S(1)} %bitcast.59, bf16[1,2,3072,1536]{3,2,1,0:T(8,128)(2,1)} %param.11), kind=kOutput, calls=%fused_computation.7 | convolution fusion | flops 9663676416 | bytes 25165824 | tf_op jit(solution)/shard_map/dot_general | solution.py:26
  182.1 15.2 %fusion.9 = f32[3072,1024]{0,1:T(8,128)} fusion(bf16[1536,1024]{0,1:T(8,128)(2,1)S(1)} %bitcast.60, bf16[1,2,3072,1536]{3,2,1,0:T(8,128)(2,1)} %param.11), kind=kOutput, calls=%fused_computation.8 | convolution fusion | flops 9663676416 | bytes 25165824 | tf_op jit(solution)/shard_map/dot_general | solution.py:27
  197.3 7.4 %fusion.13 = (f32[3072,1,512]{0,2,1:T(8,128)S(1)}, f32[3072,1,512]{0,2,1:T(8,128)}) fusion(f32[3072,1024]{0,1:T(8,128)} %fusion.9, f32[3072,1024]{0,1:T(8,128)S(1)} %fusion.6), kind=kLoop, calls=%fused_computation.12 | loop fusion | flops 3145728 | bytes 37748736 | tf_op jit(solution)/shard_map/stack | solution.py:28
  204.8 9.2 %maximum_negate_fusion = f32[3072,2,512]{0,2,1:T(8,128)} fusion(f32[3072,1,512]{0,2,1:T(8,128)} %get-tuple-element.11, f32[3072,1,512]{0,2,1:T(8,128)S(1)} %get-tuple-element.10), kind=kLoop, calls=%fused_computation | loop fusion | flops 6291456 | bytes 25165824 | tf_op jit(solution)/shard_map/neg | solution.py:28
  213.9 0.0 copy-start.4
  213.9 0.0 reduce-scatter.2.cloned.1.call-update
  214.0 0.3 all-reduce.4.cloned.1.call-start
  214.2 209.9 %reduce-scatter.2.cloned.1.call-done = f32[768,2,512]{0,2,1:T(8,128)} async-done(((f32[3072,2,512]{0,2,1:T(8,128)}), f32[768,2,512]{0,2,1:T(8,128)}) %reduce-scatter.2.cloned.1.call-update) | async-done | bytes 3145744 | tf_op jit(solution)/shard_map/reduce_scatter | solution.py:68
  424.2 0.0 copy-done.4
  424.2 7.1 %fusion.43 = f32[1024,1024]{1,0:T(8,128)S(1)} fusion(bf16[768,1024]{0,1:T(8,128)(2,1)S(1)} %bitcast.58, f32[768,1024]{0,1:T(8,128)} %bitcast.55), kind=kOutput, calls=%fused_computation.56 | convolution fusion | flops 9663676416 | bytes 8912896 | tf_op jit(solution)/shard_map/dot_general | solution.py:37
  431.3 0.5 fusion.28
  431.8 1.5 pad_maximum_fusion
  433.3 0.0 copy-start.5
  433.3 0.0 all-reduce.4.cloned.1.call-update
  433.4 0.0 all-reduce.6.cloned.1.call-start
  433.4 0.6 copy-done.5
  434.0 0.6 fusion.41
  434.6 0.0 copy-start.1
  434.6 4.7 fusion.18
  439.3 60.3 %all-reduce.4.cloned.1.call-done = f32[2,512,512]{2,1,0:T(8,128)} async-done(((f32[2,512,512]{2,1,0:T(8,128)}), f32[2,512,512]{2,1,0:T(8,128)}) %all-reduce.4.cloned.1.call-update) | async-done | bytes 2097168 | tf_op jit(solution)/shard_map/psum | solution.py:71
  499.5 0.0 copy-done.1
  499.5 2.1 bitcast_subtract_fusion
  501.6 0.0 copy-start.3
  501.6 1.3 copy-done.3
  502.9 0.0 copy-start.2
  502.9 2.8 fusion.26
  505.7 0.0 all-reduce.6.cloned.1.call-update
  505.8 0.0 copy-done.2
  505.8 3.4 copy.10
  509.1 75.0 %all-reduce.6.cloned.1.call-done = (f32[768,512]{0,1:T(8,128)}, f32[512,512]{1,0:T(8,128)}) async-done(((f32[768,512]{0,1:T(8,128)}, f32[512,512]{1,0:T(8,128)}), (f32[768,512]{0,1:T(8,128)}, f32[512,512]{1,0:T(8,128)})) %all-reduce.6.cloned.1.call-update) | async-done | bytes 2621456 | tf_op jit(solution)/shard_map/psum | solution.py:74
  584.2 1.0 constant_dynamic-slice_fusion.1
  585.2 0.9 copy.11
  586.1 1.7 constant_dynamic-slice_fusion
Async XLA Ops:
  7.2 160.4 %all-gather.2.cloned.1.call-start = ((), (), s32[]{:S(2)}) async-start(), calls=%async_computation.1 | async-start | bytes 14155776 | tf_op jit(solution)/shard_map/all_gather | solution.py:64
  33.4 5.0 copy-start
  50.4 373.8 %reduce-scatter.2.cloned.1.call-start = ((), (), s32[]{:S(2)}) async-start(), calls=%async_computation.2 | async-start | bytes 15728640 | tf_op jit(solution)/shard_map/reduce_scatter | solution.py:68
  213.9 210.2 %copy-start.4 = (bf16[768,2,512]{0,2,1:T(8,128)(2,1)S(1)}, bf16[768,2,512]{0,2,1:T(8,128)(2,1)}, u32[]{:S(2)}) copy-start(bf16[768,2,512]{0,2,1:T(8,128)(2,1)} %pad_maximum_fusion.1) | copy-start | bytes 4718596
  214.0 285.5 %all-reduce.4.cloned.1.call-start = ((), (), s32[]{:S(2)}) async-start(), calls=%async_computation.3 | async-start | bytes 4194304 | tf_op jit(solution)/shard_map/psum | solution.py:71
  433.3 0.7 copy-start.5
  433.4 150.8 %all-reduce.6.cloned.1.call-start = ((), (), s32[]{:S(2)}) async-start(), calls=%async_computation.4 | async-start | bytes 5242880 | tf_op jit(solution)/shard_map/psum | solution.py:74
  434.6 64.9 %copy-start.1 = (f32[1,2,512,512]{3,2,1,0:T(8,128)S(1)}, f32[1,2,512,512]{3,2,1,0:T(8,128)}, u32[]{:S(2)}) copy-start(f32[1,2,512,512]{3,2,1,0:T(8,128)} %param.10) | copy-start | bytes 6291460
  501.6 1.3 copy-start.3
  502.9 2.9 copy-start.2
Sparse Core Ops, SparseCore 0:
  50.5 116.9 all-gather.1
  214.1 210.0 reduce-scatter.1
  433.5 65.9 all-reduce.3
  505.9 78.2 all-reduce.5
where the time goes:
time: 595 us; the launch traced here: 594 us
  waiting for transfers between devices  462 us (78%)
  matrix products  49.6 us (8%)
  other arithmetic  29.7 us (5%)
  blocking collectives  24.9 us (4%)
  between operations  14.5 us (2%)
  local copies, waits for them, and re-layouts  12.9 us (2%)
    reduce_scatter x1, waiting for transfers between devices, body(): lax.psum_scatter(apply_block(block_real, block_imag, needed), 'col', scat...  210 us
    all_gather x1, waiting for transfers between devices, body(): gathered = lax.all_gather(owned, ('row', 'col'), axis=0, tiled=True)  117 us
    psum x1, waiting for transfers between devices, body(): totals = lax.psum((column_density, pivot_density), 'pole')  75 us
    psum x1, waiting for transfers between devices, body(): pivot = inverse - lax.psum(pivot_term(owned, column), ('row', 'col'))  60.3 us
    dot_general x1, matrix products, apply_block(): second = jnp.dot(block_imag, flat, preferred_element_type=jnp.float32)  15.2 us
    dot_general x4, matrix products, precise(): jnp.dot(left, right, precision=lax.Precision.HIGHEST, preferred_element_t...  14.8 us
    all_gather x1, blocking collectives, body(): lax.all_gather(margin_panel, 'pole', axis=1, tiled=True)  13.8 us
    dot_general x1, matrix products, apply_block(): first = jnp.dot(block_real, flat, preferred_element_type=jnp.float32)  12.5 us
  transfers between devices with their start and end apart: 4, of which 4 were waited for; matrix products, arithmetic and copies ran while one was open for 1% of the time, Pallas kernels for 0%

commit v1 on v0

v1 whole, which is shorter than its diff:
```python
import jax
import jax.numpy as jnp
from jax import lax
from jax.sharding import PartitionSpec as P

HALVES = 2


def precise(left, right):
    return jnp.dot(left, right, precision=lax.Precision.HIGH, preferred_element_type=jnp.float32)


def gather_panel(pair):
    return lax.all_gather(pair, "pole", axis=2, tiled=True)


def factor_panel(pair, shift, inverse):
    hamiltonian_f = pair[0].astype(jnp.float32)
    margin_f = pair[1].astype(jnp.float32)
    real_part = hamiltonian_f - shift[0] * margin_f
    imag_part = -shift[1] * margin_f
    lower_real = precise(real_part, inverse[0]) - precise(imag_part, inverse[1])
    lower_imag = precise(real_part, inverse[1]) + precise(imag_part, inverse[0])
    return lower_real.astype(jnp.bfloat16), lower_imag.astype(jnp.bfloat16)


def half_dot(left, right):
    return lax.dot_general(
        left, right, (((0,), (0,)), ((), ())), preferred_element_type=jnp.float32
    )


def body(hamiltonian_panel, margin_panel, shifts, weights, pivot_inverse, selected_inverse):
    shift = shifts[0]
    weight = weights[0]
    inverse = pivot_inverse[0]
    block_real = selected_inverse[0, 0]
    block_imag = selected_inverse[0, 1]
    n_row = lax.axis_size("row")
    n_col = lax.axis_size("col")
    n_pole = lax.axis_size("pole")
    width = inverse.shape[-1]
    part = width // HALVES

    own_pair = jnp.stack([hamiltonian_panel, margin_panel])
    order = [(n_row * c + r, r * n_col + c) for r in range(n_row) for c in range(n_col)]
    met_pair = gather_panel(lax.ppermute(own_pair, ("row", "col"), order))
    met_real, met_imag = factor_panel(met_pair, shift, inverse)

    partials = []
    for h in range(HALVES):
        cut = slice(h * part, (h + 1) * part)
        mine = jnp.concatenate([met_real[:, cut], met_imag[:, cut]], axis=1)
        rows = lax.all_gather(mine, "row", axis=0, tiled=True)
        turned = jnp.concatenate([rows[:, part:], -rows[:, :part]], axis=1)
        total = jnp.dot(block_imag, turned, preferred_element_type=jnp.float32) - jnp.dot(
            block_real, rows, preferred_element_type=jnp.float32
        )
        partials.append(total.astype(jnp.bfloat16))

    own_pair, partials[-1] = lax.optimization_barrier((own_pair, partials[-1]))
    own_real, own_imag = factor_panel(gather_panel(own_pair), shift, inverse)
    lower = jnp.concatenate([own_real, own_imag], axis=1)

    columns = []
    updates = []
    for h in range(HALVES):
        column = lax.psum_scatter(
            partials[h], "col", scatter_dimension=0, tiled=True
        ).astype(jnp.float32)
        high = column.astype(jnp.bfloat16)
        low = (column - high.astype(jnp.float32)).astype(jnp.bfloat16)
        square = half_dot(lower, high) + half_dot(lower, low)
        update = jnp.stack(
            [
                square[:width, :part] - square[width:, part:],
                square[:width, part:] + square[width:, :part],
            ]
        )
        updates.append(lax.psum(update, ("row", "col")))
        columns.append(column.reshape(column.shape[0], 2, part))
    column = jnp.concatenate(columns, axis=2)
    pivot = inverse - jnp.concatenate(updates, axis=2)

    column_density = weight[0] * column[:, 0] - weight[1] * column[:, 1]
    share = width // n_pole
    pieces = column_density.reshape(-1, n_pole, share).swapaxes(0, 1).astype(jnp.bfloat16)
    column_share = jnp.sum(
        lax.all_to_all(pieces, "pole", 0, 0, tiled=True).astype(jnp.float32), axis=0
    )
    pivot_density = weight[0] * pivot[0] - weight[1] * pivot[1]
    pieces = pivot_density.reshape(n_pole, share, width).astype(jnp.bfloat16)
    pivot_share = jnp.sum(
        lax.all_to_all(pieces, "pole", 0, 0, tiled=True).astype(jnp.float32), axis=0
    )
    return (column[None], pivot[None], column_share, pivot_share)


def solution(mesh):
    return jax.shard_map(
        body,
        mesh=mesh,
        in_specs=(
            P(("row", "col"), "pole"),
            P(("row", "col"), "pole"),
            P("pole", None),
            P("pole", None),
            P("pole", None, None, None),
            P("pole", None, "row", "col"),
        ),
        out_specs=(
            P("pole", ("row", "col"), None, None),
            P("pole", None, None, None),
            P(("row", "col"), "pole"),
            P("pole", None),
        ),
        check_vma=False,
    )
```

time: 595 us -> 351 us (0.59)
  waiting for transfers between devices: 462 us -> 223 us
  blocking collectives: 24.9 us -> 0 us
  matrix products: 49.6 us -> 66.5 us
  starting transfers between devices: 0.38 us -> 9.61 us
    reduce_scatter x1 -> x2, waiting for transfers between devices: 210 us -> 112 us  [body(): lax.psum_scatter(partials[h], 'col', scatter_dimension=0, tiled=True)]
    psum x2 -> x1, waiting for transfers between devices: 135 us -> 45.3 us  [body(): updates.append(lax.psum(update, ('row', 'col')))]
    all_gather x1 -> x4, waiting for transfers between devices: 117 us -> 62.9 us  [the longest x2 54 us: gather_panel(): return lax.all_gather(pair, 'pole', axis=2, tiled=True)]
    all_gather x2 -> x0, blocking collectives: 24.9 us -> none  [the longest x1 13.8 us: body(): lax.all_gather(margin_panel, 'pole', axis=1, tiled=True)]
    dot_general x7 -> x16, matrix products: 49.6 us -> 66.5 us  [the longest x2 21.5 us: body(): jnp.dot(block_imag, turned, preferred_element_type=jnp.float32)]
    neg x1 -> x0, other arithmetic: 9.17 us -> none  [apply_block(): -jnp.stack([first[:, :width] - second[:, width:], first[:, width:] + seco...]
    all_to_all x0 -> x2, starting transfers between devices: none -> 8.46 us  [body(): lax.all_to_all(pieces, 'pole', 0, 0, tiled=True).astype(jnp.float32)]
    another operation x4 -> x5, other arithmetic: 10.9 us -> 3.51 us  [the longest x4 2.45 us: body(): jnp.stack([square[:width, :part] - square[width:, part:], square[:width,...]
  transfers between devices with their start and end apart: 4 -> 10, of which waited for: 4 -> 7; matrix products, arithmetic and copies ran while one was open for 1% -> 22% of each run, Pallas kernels for 0% -> 0%
where the time goes in v1:
time: 351 us; the launch traced here: 350 us
  waiting for transfers between devices  223 us (64%)
  matrix products  66.5 us (19%)
  other arithmetic  23.8 us (7%)
  between operations  15.1 us (4%)
  local copies, waits for them, and re-layouts  12.5 us (4%)
  starting transfers between devices  9.61 us (3%)
    reduce_scatter x2, waiting for transfers between devices, body(): lax.psum_scatter(partials[h], 'col', scatter_dimension=0, tiled=True)  112 us
    all_gather x2, waiting for transfers between devices, gather_panel(): return lax.all_gather(pair, 'pole', axis=2, tiled=True)  54 us
    psum x1, waiting for transfers between devices, body(): updates.append(lax.psum(update, ('row', 'col')))  45.3 us
    dot_general x2, matrix products, body(): jnp.dot(block_imag, turned, preferred_element_type=jnp.float32)  21.5 us
    dot_general x8, matrix products, precise(): jnp.dot(left, right, precision=lax.Precision.HIGH, preferred_element_type...  20.8 us
    dot_general x2, matrix products, body(): jnp.dot(block_real, rows, preferred_element_type=jnp.float32)  16.9 us
    unnamed x40, local copies, waits for them, and re-layouts  10.5 us
    all_gather x2, waiting for transfers between devices, body(): rows = lax.all_gather(mine, 'row', axis=0, tiled=True)  8.9 us
  transfers between devices with their start and end apart: 10, of which 7 were waited for; matrix products, arithmetic and copies ran while one was open for 22% of the time, Pallas kernels for 0%

profile of v1, /device:TPU:0, one launch (start us, length us, event | category | flops | bytes accessed | tf_op | source)
XLA Modules:
  0.0 350.2 jit_solution(6100513097827890616)
XLA Ops:
  7.2 0.0 all-gather.5.cloned.1.call-start
  7.2 1.1 pad_maximum_fusion.6
  8.3 0.7 collective-permute-start
  9.0 0.7 copy-done.17
  9.8 0.0 all-gather.9.cloned.1.call-start
  9.8 1.3 fusion.112
  11.8 42.8 %all-gather.5.cloned.1.call-done = bf16[2,768,512]{2,1,0:T(8,128)(2,1)} async-done(((bf16[2,768,128]{2,1,0:T(8,128)(2,1)}), bf16[2,768,512]{2,1,0:T(8,128)(2,1)}) %all-gather.5.cloned.1.call-update) | async-done | bytes 1572880 | tf_op jit(solution)/shard_map/all_gather | solution.py:14
  54.6 3.2 fusion.28
  57.9 2.9 fusion.26
  60.7 2.3 subtract_convert_fusion.5
  63.0 2.3 add_convert_fusion.1
  65.3 0.1 fusion.109
  65.4 0.9 pad_maximum_fusion.5
  66.4 0.0 all-gather.7.cloned.1.call-start
  66.4 1.0 pad_maximum_fusion.4
  67.4 0.0 all-gather.11.cloned.1.call-start
  67.5 8.9 %all-gather.9.cloned.1.call-done = bf16[1536,512]{0,1:T(8,128)(2,1)} async-done(((bf16[768,512]{0,1:T(8,128)(2,1)}), bf16[1536,512]{0,1:T(8,128)(2,1)}) %all-gather.9.cloned.1.call-update) | async-done | bytes 1572880 | tf_op jit(solution)/shard_map/all_gather | solution.py:54
  76.3 9.2 %fusion = f32[512,3072]{1,0:T(8,128)S(1)} fusion(bf16[1536,512]{0,1:T(8,128)(2,1)} %all-gather.9.cloned.1.call-done, bf16[1,2,3072,1536]{3,2,1,0:T(8,128)(2,1)} %param.11), kind=kOutput, calls=%fused_computation | convolution fusion | flops 4831838208 | bytes 17301504 | tf_op jit(solution)/shard_map/dot_general | solution.py:56
  85.6 0.1 fusion.108
  85.7 11.0 %fusion.19 = bf16[3072,512]{0,1:T(8,128)(2,1)} fusion(f32[512,3072]{1,0:T(8,128)S(1)} %fusion, bf16[1,2,3072,1536]{3,2,1,0:T(8,128)(2,1)} %param.11, bf16[1536,256]{0,1:T(8,128)(2,1)S(1)} %get-tuple-element.25, bf16[1536,256]{0,1:T(8,128)(2,1)S(1)} %get-tuple-element.24), kind=kOutput, calls=%fused_computation.20 | convolution fusion | flops 4838129664 | bytes 20447232 | tf_op jit(solution)/shard_map/dot_general | solution.py:56
  96.7 0.0 reduce-scatter.5.cloned.1.call-start
  96.7 0.5 reduce-scatter.5.cloned.1.call-update
  97.3 0.2 reduce-scatter.3.cloned.1.call-start
  97.5 0.0 all-gather.7.cloned.1.call-done
  97.5 1.6 fusion.107
  99.1 0.3 copy-done.6
  99.4 7.7 %fusion.2 = f32[512,3072]{1,0:T(8,128)S(1)} fusion(bf16[1536,512]{0,1:T(8,128)(2,1)S(1)} %copy-done.6, bf16[1,2,3072,1536]{3,2,1,0:T(8,128)(2,1)} %param.11), kind=kOutput, calls=%fused_computation.2 | convolution fusion | flops 4831838208 | bytes 17301504 | tf_op jit(solution)/shard_map/dot_general | solution.py:56
  107.1 10.6 %fusion.16 = bf16[3072,512]{0,1:T(8,128)(2,1)} fusion(f32[512,3072]{1,0:T(8,128)S(1)} %fusion.2, bf16[1,2,3072,1536]{3,2,1,0:T(8,128)(2,1)} %param.11, bf16[1536,256]{0,1:T(8,128)(2,1)S(1)} %get-tuple-element.23, bf16[1536,256]{0,1:T(8,128)(2,1)S(1)} %get-tuple-element.22), kind=kOutput, calls=%fused_computation.19 | convolution fusion | flops 4838129664 | bytes 20447232 | tf_op jit(solution)/shard_map/dot_general | solution.py:56
  117.7 0.0 all-reduce.3.cloned.1.call-start
  117.7 11.2 %all-gather.11.cloned.1.call-done = bf16[2,768,512]{2,1,0:T(8,128)(2,1)} async-done(((bf16[2,768,128]{2,1,0:T(8,128)(2,1)}), bf16[2,768,512]{2,1,0:T(8,128)(2,1)}) %all-gather.11.cloned.1.call-update) | async-done | bytes 1572880 | tf_op jit(solution)/shard_map/all_gather | solution.py:14
  128.9 3.7 %fusion.53 = f32[768,512]{0,1:T(8,128)S(1)} fusion(f32[1,2,512,512]{3,2,1,0:T(8,128)S(1)} %copy-done, f32[]{:T(128)} %bitcast.2, bf16[2,768,512]{2,1,0:T(8,128)(2,1)} %all-gather.11.cloned.1.call-done), kind=kOutput, calls=%fused_computation.60 | convolution fusion | flops 1209532416 | bytes 4194308 | tf_op jit(solution)/shard_map/dot_general | solution.py:10
  132.6 2.3 fusion.55
  134.9 1.6 add_convert_fusion
  136.6 2.5 subtract_convert_fusion.4
  139.1 52.8 %reduce-scatter.5.cloned.1.call-done = bf16[768,512]{0,1:T(8,128)(2,1)} async-done(((bf16[3072,512]{0,1:T(8,128)(2,1)}), bf16[768,512]{0,1:T(8,128)(2,1)}) %reduce-scatter.5.cloned.1.call-update) | async-done | bytes 786448 | tf_op jit(solution)/shard_map/reduce_scatter | solution.py:68
  191.9 2.5 fusion.105
  194.4 1.0 convolution_add_fusion
  195.5 0.1 fusion.90
  195.6 58.8 %reduce-scatter.3.cloned.1.call-done = bf16[768,512]{0,1:T(8,128)(2,1)} async-done(((bf16[3072,512]{0,1:T(8,128)(2,1)}), bf16[768,512]{0,1:T(8,128)(2,1)}) %reduce-scatter.3.cloned.1.call-update) | async-done | bytes 786448 | tf_op jit(solution)/shard_map/reduce_scatter | solution.py:68
  254.4 2.8 fusion.106
  257.2 1.0 convolution_add_fusion.1
  258.2 0.1 fusion.92
  258.3 1.1 pad_maximum_fusion.3
  259.4 1.1 pad_maximum_fusion.2
  260.5 0.6 copy-done.18
  261.2 0.6 fusion.111
  261.8 0.1 convert
  261.9 0.5 copy-done.16
  262.4 0.1 convert.1
  262.5 0.5 copy-done.1
  263.0 1.1 copy-done.2
  264.2 1.8 fusion.22
  266.0 5.7 %copy.13 = f32[1,768,2,512]{3,2,1,0:T(2,128)} copy(f32[1,768,2,512]{1,3,2,0:T(8,128)} %fusion.22) | data formatting | bytes 6291456
  271.7 4.3 %fusion.40 = bf16[768,1,512]{0,2,1:T(8,128)(2,1)} fusion(f32[768,2,256]{0,2,1:T(8,128)} %copy-done.2, f32[768,2,256]{0,2,1:T(8,128)} %copy-done.1, f32[]{:T(128)} %bitcast.24, f32[]{:T(128)} %bitcast.23), kind=kLoop, calls=%fused_computation.43 | loop fusion | flops 2359296 | bytes 3932168 | tf_op jit(solution)/shard_map/convert_element_type | solution.py:87
  276.0 4.2 %all-to-all-start = ((bf16[4,768,128]{1,2,0:T(8,128)(2,1)}), bf16[4,768,128]{1,2,0:T(8,128)(2,1)}, u32[]{:S(2)}, u32[]{:S(2)}) async-start(bf16[4,768,128]{1,2,0:T(8,128)(2,1)} %bitcast.26), calls=%async_computation.2 | async-start | bytes 1572864 | tf_op jit(solution)/shard_map/all_to_all | solution.py:89
  280.2 45.3 %all-reduce.3.cloned.1.call-done = (f32[2,512,256]{2,1,0:T(8,128)}, f32[2,512,256]{2,1,0:T(8,128)}) async-done(((f32[2,512,256]{2,1,0:T(8,128)}, f32[2,512,256]{2,1,0:T(8,128)}), (f32[2,512,256]{2,1,0:T(8,128)}, f32[2,512,256]{2,1,0:T(8,128)})) %all-reduce.3.cloned.1.call-update) | async-done | bytes 2097168 | tf_op jit(solution)/shard_map/psum | solution.py:80
  325.5 2.0 maximum_subtract_fusion.1
  327.5 2.4 fusion.60
  329.9 4.3 %all-to-all-start.1 = ((bf16[4,128,512]{2,1,0:T(8,128)(2,1)}), bf16[4,128,512]{2,1,0:T(8,128)(2,1)}, u32[]{:S(2)}, u32[]{:S(2)}) async-start(bf16[4,128,512]{2,1,0:T(8,128)(2,1)} %bitcast.94), calls=%async_computation.3 | async-start | bytes 1048576 | tf_op jit(solution)/shard_map/all_to_all | solution.py:94
  334.2 1.3 convert_reduce_fusion
  335.5 0.9 copy.14
  336.4 2.9 maximum_subtract_fusion
  339.3 2.2 all-to-all-done.1
  341.5 1.8 convert_reduce_fusion.1
  (40 shorter events, 0.2 us)
Async XLA Ops:
  7.2 47.4 %all-gather.5.cloned.1.call-start = ((), (), s32[]{:S(2)}) async-start(), calls=%async_computation.4 | async-start | bytes 1966080 | tf_op jit(solution)/shard_map/all_gather | solution.py:14
  8.3 49.6 %copy-start.8 = (bf16[2,768,128]{2,1,0:T(8,128)(2,1)}, bf16[2,768,128]{2,1,0:T(8,128)(2,1)S(1)}, u32[]{:S(2)}) copy-start(bf16[2,768,128]{2,1,0:T(8,128)(2,1)S(1)} %pad_maximum_fusion.6) | copy-start | bytes 1179652
  8.3 0.7 collective-permute-start
  9.0 0.7 copy-start.17
  9.8 66.6 %all-gather.9.cloned.1.call-start = ((), (), s32[]{:S(2)}) async-start(), calls=%async_computation.7 | async-start | bytes 2359296 | tf_op jit(solution)/shard_map/all_gather | solution.py:54
  54.6 3.2 copy-start
  57.9 2.9 copy-start.4
  66.4 31.1 %all-gather.7.cloned.1.call-start = ((), (), s32[]{:S(2)}) async-start(), calls=%async_computation.5 | async-start | bytes 2359296 | tf_op jit(solution)/shard_map/all_gather | solution.py:54
  67.4 61.5 %all-gather.11.cloned.1.call-start = ((), (), s32[]{:S(2)}) async-start(), calls=%async_computation.9 | async-start | bytes 1966080 | tf_op jit(solution)/shard_map/all_gather | solution.py:14
  76.3 9.2 %copy-start.7 = (bf16[1536,512]{0,1:T(8,128)(2,1)S(1)}, bf16[1536,512]{0,1:T(8,128)(2,1)}, u32[]{:S(2)}) copy-start(bf16[1536,512]{0,1:T(8,128)(2,1)} %all-gather.9.cloned.1.call-done) | copy-start | bytes 4718596
  96.7 95.2 %reduce-scatter.5.cloned.1.call-start = ((), (), s32[]{:S(2)}) async-start(), calls=%async_computation.8 | async-start | bytes 3932160 | tf_op jit(solution)/shard_map/reduce_scatter | solution.py:68
  97.3 157.1 %reduce-scatter.3.cloned.1.call-start = ((), (), s32[]{:S(2)}) async-start(), calls=%async_computation.6 | async-start | bytes 3932160 | tf_op jit(solution)/shard_map/reduce_scatter | solution.py:68
  97.5 1.9 copy-start.6
  117.7 207.9 %all-reduce.3.cloned.1.call-start = ((), (), s32[]{:S(2)}) async-start(), calls=%async_computation.10 | async-start | bytes 4194304 | tf_op jit(solution)/shard_map/psum | solution.py:80
  128.9 3.8 %copy-start.3 = (bf16[2,768,512]{2,1,0:T(8,128)(2,1)S(1)}, bf16[2,768,512]{2,1,0:T(8,128)(2,1)}, u32[]{:S(2)}) copy-start(bf16[2,768,512]{2,1,0:T(8,128)(2,1)} %all-gather.11.cloned.1.call-done) | copy-start | bytes 4718596
  136.6 57.8 %copy-start.9 = (bf16[768,512]{0,1:T(8,128)(2,1)}, bf16[768,512]{0,1:T(8,128)(2,1)S(1)}, u32[]{:S(2)}) copy-start(bf16[768,512]{0,1:T(8,128)(2,1)S(1)} %add_convert_fusion) | copy-start | bytes 2359300
  191.9 2.5 copy-start.11
  191.9 2.5 copy-start.13
  254.4 2.8 copy-start.10
  254.4 2.8 copy-start.12
  254.4 2.8 copy-start.15
  260.5 0.7 copy-start.18
  260.5 1.2 copy-start.14
  261.2 1.2 copy-start.16
  261.9 1.1 copy-start.1
  263.0 1.1 copy-start.2
  276.0 53.9 %all-to-all-start = ((bf16[4,768,128]{1,2,0:T(8,128)(2,1)}), bf16[4,768,128]{1,2,0:T(8,128)(2,1)}, u32[]{:S(2)}, u32[]{:S(2)}) async-start(bf16[4,768,128]{1,2,0:T(8,128)(2,1)} %bitcast.26), calls=%async_computation.2 | async-start | bytes 1572864 | tf_op jit(solution)/shard_map/all_to_all | solution.py:89
  329.9 6.5 %copy-start.5 = (f32[2,512,256]{2,1,0:T(8,128)S(1)}, f32[2,512,256]{2,1,0:T(8,128)}, u32[]{:S(2)}) copy-start(f32[2,512,256]{2,1,0:T(8,128)} %get-tuple-element.16) | copy-start | bytes 3145732
  329.9 11.6 %all-to-all-start.1 = ((bf16[4,128,512]{2,1,0:T(8,128)(2,1)}), bf16[4,128,512]{2,1,0:T(8,128)(2,1)}, u32[]{:S(2)}, u32[]{:S(2)}) async-start(bf16[4,128,512]{2,1,0:T(8,128)(2,1)} %bitcast.94), calls=%async_computation.3 | async-start | bytes 1048576 | tf_op jit(solution)/shard_map/all_to_all | solution.py:94
Sparse Core Ops, SparseCore 0:
  10.4 44.1 all-gather.4
  66.5 9.7 all-gather.8
  77.9 10.9 all-gather.6
  96.8 32.0 all-gather.10
  131.6 60.2 reduce-scatter.4
  194.0 60.2 reduce-scatter.2
  260.7 64.8 all-reduce.2

commit v2 on v1

--- a/solution.py
+++ b/solution.py
@@ -11,7 +11,15 @@
 
 
 def gather_panel(pair):
-    return lax.all_gather(pair, "pole", axis=2, tiled=True)
+    rows = pair.shape[0] // 2
+    return (
+        lax.all_gather(pair[:rows], "pole", axis=1, tiled=True),
+        lax.all_gather(pair[rows:], "pole", axis=1, tiled=True),
+    )
+
+
+def exchange_sum(pieces, axis):
+    return jnp.sum(lax.all_to_all(pieces, axis, 0, 0, tiled=True).astype(jnp.float32), axis=0)
 
 
 def factor_panel(pair, shift, inverse):
@@ -42,7 +50,7 @@
     width = inverse.shape[-1]
     part = width // HALVES
 
-    own_pair = jnp.stack([hamiltonian_panel, margin_panel])
+    own_pair = jnp.concatenate([hamiltonian_panel, margin_panel], axis=0)
     order = [(n_row * c + r, r * n_col + c) for r in range(n_row) for c in range(n_col)]
     met_pair = gather_panel(lax.ppermute(own_pair, ("row", "col"), order))
     met_real, met_imag = factor_panel(met_pair, shift, inverse)
@@ -65,9 +73,7 @@
     columns = []
     updates = []
     for h in range(HALVES):
-        column = lax.psum_scatter(
-            partials[h], "col", scatter_dimension=0, tiled=True
-        ).astype(jnp.float32)
+        column = exchange_sum(partials[h].reshape(n_col, -1, 2 * part), "col")
         high = column.astype(jnp.bfloat16)
         low = (column - high.astype(jnp.float32)).astype(jnp.bfloat16)
         square = half_dot(lower, high) + half_dot(lower, low)
@@ -77,22 +83,22 @@
                 square[:width, part:] + square[width:, :part],
             ]
         )
-        updates.append(lax.psum(update, ("row", "col")))
+        updates.append(update)
         columns.append(column.reshape(column.shape[0], 2, part))
     column = jnp.concatenate(columns, axis=2)
-    pivot = inverse - jnp.concatenate(updates, axis=2)
+    update = jnp.concatenate(updates, axis=2)
+    pieces = update.reshape(n_row * n_col, -1, width).astype(jnp.bfloat16)
+    piece = lax.optimization_barrier(exchange_sum(pieces, ("row", "col")))
+    update = lax.all_gather(piece.astype(jnp.bfloat16), ("row", "col"), axis=0, tiled=True)
+    pivot = inverse - update.reshape(2, width, width).astype(jnp.float32)
 
     column_density = weight[0] * column[:, 0] - weight[1] * column[:, 1]
     share = width // n_pole
-    pieces = column_density.reshape(-1, n_pole, share).swapaxes(0, 1).astype(jnp.bfloat16)
-    column_share = jnp.sum(
-        lax.all_to_all(pieces, "pole", 0, 0, tiled=True).astype(jnp.float32), axis=0
+    column_share = exchange_sum(
+        column_density.reshape(-1, n_pole, share).swapaxes(0, 1), "pole"
     )
     pivot_density = weight[0] * pivot[0] - weight[1] * pivot[1]
-    pieces = pivot_density.reshape(n_pole, share, width).astype(jnp.bfloat16)
-    pivot_share = jnp.sum(
-        lax.all_to_all(pieces, "pole", 0, 0, tiled=True).astype(jnp.float32), axis=0
-    )
+    pivot_share = exchange_sum(pivot_density.reshape(n_pole, share, width), "pole")
     return (column[None], pivot[None], column_share, pivot_share)
 
 

time: 351 us -> 333 us (0.949)
  waiting for transfers between devices: 223 us -> 119 us
  blocking collectives: 0 us -> 78.1 us
  matrix products: 66.5 us -> 50.3 us
  starting transfers between devices: 9.61 us -> 18.2 us
  local copies, waits for them, and re-layouts: 12.5 us -> 20.5 us
  other arithmetic: 23.8 us -> 31.3 us
    reduce_scatter x2 -> x0, waiting for transfers between devices: 112 us -> none  [body(): lax.psum_scatter(partials[h], 'col', scatter_dimension=0, tiled=True)]
    all_to_all x2 -> x4, waiting for transfers between devices: 2.24 us -> 77.5 us  [exchange_sum(): lax.all_to_all(pieces, axis, 0, 0, tiled=True).astype(jnp.float32)]
    all_gather x0 -> x4, blocking collectives: none -> 48.3 us  [the longest x2 24.3 us: gather_panel(): lax.all_gather(pair[:rows], 'pole', axis=1, tiled=True)]
    all_gather x2 -> x1, waiting for transfers between devices: 54 us -> 8.52 us  [body(): lax.all_gather(piece.astype(jnp.bfloat16), ('row', 'col'), axis=0, tiled=...]
    psum x1 -> x0, waiting for transfers between devices: 45.3 us -> none  [body(): updates.append(lax.psum(update, ('row', 'col')))]
    all_to_all x0 -> x1, blocking collectives: none -> 29.8 us  [exchange_sum(): lax.all_to_all(pieces, axis, 0, 0, tiled=True).astype(jnp.float32)]
    all_gather x2, waiting for transfers between devices: 8.9 us -> 33.1 us  [body(): rows = lax.all_gather(mine, 'row', axis=0, tiled=True)]
    all_to_all x2 -> x4, starting transfers between devices: 8.46 us -> 17.4 us  [exchange_sum(): lax.all_to_all(pieces, axis, 0, 0, tiled=True).astype(jnp.float32)]
  transfers between devices with their start and end apart: 10 -> 8, of which waited for: 7 -> 6; matrix products, arithmetic and copies ran while one was open for 22% -> 19% of each run, Pallas kernels for 0% -> 0%
where the time goes in v2:
time: 333 us; the launch traced here: 332 us
  waiting for transfers between devices  119 us (36%)
  blocking collectives  78.1 us (23%)
  matrix products  50.3 us (15%)
  other arithmetic  31.3 us (9%)
  local copies, waits for them, and re-layouts  20.5 us (6%)
  starting transfers between devices  18.2 us (5%)
  between operations  14.7 us (4%)
    all_to_all x4, waiting for transfers between devices, exchange_sum(): lax.all_to_all(pieces, axis, 0, 0, tiled=True).astype(jnp.float32)  77.5 us
    all_gather x2, waiting for transfers between devices, body(): rows = lax.all_gather(mine, 'row', axis=0, tiled=True)  33.1 us
    all_to_all x1, blocking collectives, exchange_sum(): lax.all_to_all(pieces, axis, 0, 0, tiled=True).astype(jnp.float32)  29.8 us
    all_gather x2, blocking collectives, gather_panel(): lax.all_gather(pair[:rows], 'pole', axis=1, tiled=True)  24.3 us
    all_gather x2, blocking collectives, gather_panel(): lax.all_gather(pair[rows:], 'pole', axis=1, tiled=True)  24 us
    all_to_all x4, starting transfers between devices, exchange_sum(): lax.all_to_all(pieces, axis, 0, 0, tiled=True).astype(jnp.float32)  17.4 us
    dot_general x8, matrix products, precise(): jnp.dot(left, right, precision=lax.Precision.HIGH, preferred_element_type...  15.6 us
    dot_general x2, matrix products, body(): jnp.dot(block_real, rows, preferred_element_type=jnp.float32)  15.3 us
  transfers between devices with their start and end apart: 8, of which 6 were waited for; matrix products, arithmetic and copies ran while one was open for 19% of the time, Pallas kernels for 0%

profile of v2, /device:TPU:0, one launch (start us, length us, event | category | flops | bytes accessed | tf_op | source)
XLA Modules:
  0.0 332.2 jit_solution(18348677781217761953)
XLA Ops:
  7.2 1.1 constant_dynamic-update-slice_fusion.1
  8.3 1.0 constant_dynamic-update-slice_fusion
  9.3 0.7 collective-permute-start
  10.0 1.3 fusion.91
  12.0 12.6 %all_gather.22 = bf16[768,512]{1,0:T(8,128)(2,1)S(1)} all-gather(bf16[768,128]{1,0:T(8,128)(2,1)S(1)} %get-tuple-element.27), channel_id=1, replica_groups=mesh['pole'=4,'row'=2,'col'=4] {'pole'}, dimensions={1}, use_global_device_ids=true | all-gather | bytes 983040 | tf_op jit(solution)/shard_map/all_gather | solution.py:17
  24.5 1.6 fusion.21
  26.2 1.6 fusion.20
  27.8 12.2 %all_gather.21 = bf16[768,512]{1,0:T(8,128)(2,1)S(1)} all-gather(bf16[768,128]{1,0:T(8,128)(2,1)S(1)} %get-tuple-element.26), channel_id=1, replica_groups=mesh['pole'=4,'row'=2,'col'=4] {'pole'}, dimensions={1}, use_global_device_ids=true | all-gather | bytes 983040 | tf_op jit(solution)/shard_map/all_gather | solution.py:16
  40.0 2.3 subtract_convert_fusion.5
  42.3 2.3 add_convert_fusion.1
  44.6 0.1 fusion.86
  44.7 0.9 pad_maximum_fusion.3
  45.7 19.8 %all-gather.6.cloned.1.call-done = bf16[1536,512]{0,1:T(8,128)(2,1)} async-done(((bf16[768,512]{0,1:T(8,128)(2,1)}), bf16[1536,512]{0,1:T(8,128)(2,1)}) %all-gather.6.cloned.1.call-update) | async-done | bytes 1572880 | tf_op jit(solution)/shard_map/all_gather | solution.py:62
  65.5 1.6 fusion.85
  67.1 0.3 copy-done.6
  67.4 7.7 %fusion = f32[512,3072]{1,0:T(8,128)S(1)} fusion(bf16[1536,512]{0,1:T(8,128)(2,1)S(1)} %copy-done.6, bf16[1,2,3072,1536]{3,2,1,0:T(8,128)(2,1)} %param.11), kind=kOutput, calls=%fused_computation | convolution fusion | flops 4831838208 | bytes 17301504 | tf_op jit(solution)/shard_map/dot_general | solution.py:64
  75.1 7.6 %fusion.16 = bf16[3072,512]{0,1:T(8,128)(2,1)S(1)} fusion(f32[512,3072]{1,0:T(8,128)S(1)} %fusion, bf16[1,2,3072,1536]{3,2,1,0:T(8,128)(2,1)} %param.11, bf16[1536,256]{0,1:T(8,128)(2,1)S(1)} %get-tuple-element.19, bf16[1536,256]{0,1:T(8,128)(2,1)S(1)} %get-tuple-element.18), kind=kOutput, calls=%fused_computation.21 | convolution fusion | flops 4838129664 | bytes 20447232 | tf_op jit(solution)/shard_map/dot_general | solution.py:64
  82.7 1.9 copy.31
  84.6 4.9 %all-to-all-start.1 = ((bf16[4,768,512]{1,2,0:T(8,128)(2,1)}), bf16[4,768,512]{1,2,0:T(8,128)(2,1)}, u32[]{:S(2)}, u32[]{:S(2)}) async-start(bf16[4,768,512]{1,2,0:T(8,128)(2,1)} %bitcast.79), calls=%async_computation.1 | async-start | bytes 6291456 | tf_op jit(solution)/shard_map/all_to_all | solution.py:22
  89.5 0.9 pad_maximum_fusion.2
  90.4 13.2 %all-gather.4.cloned.1.call-done = bf16[1536,512]{0,1:T(8,128)(2,1)} async-done(((bf16[768,512]{0,1:T(8,128)(2,1)}), bf16[1536,512]{0,1:T(8,128)(2,1)}) %all-gather.4.cloned.1.call-update) | async-done | bytes 1572880 | tf_op jit(solution)/shard_map/all_gather | solution.py:62
  103.7 1.6 fusion.84
  105.3 0.3 copy-done.7
  105.5 7.7 %fusion.2 = f32[512,3072]{1,0:T(8,128)S(1)} fusion(bf16[1536,512]{0,1:T(8,128)(2,1)S(1)} %copy-done.7, bf16[1,2,3072,1536]{3,2,1,0:T(8,128)(2,1)} %param.11), kind=kOutput, calls=%fused_computation.2 | convolution fusion | flops 4831838208 | bytes 17301504 | tf_op jit(solution)/shard_map/dot_general | solution.py:64
  113.2 7.6 %subtract_convert_fusion.1 = bf16[512,3072]{1,0:T(8,128)(2,1)S(1)} fusion(f32[512,3072]{1,0:T(8,128)S(1)} %fusion.2, bf16[1,2,3072,1536]{3,2,1,0:T(8,128)(2,1)} %param.11, bf16[1536,256]{0,1:T(8,128)(2,1)S(1)} %get-tuple-element.17, bf16[1536,256]{0,1:T(8,128)(2,1)S(1)} %get-tuple-element.16), kind=kOutput, calls=%fused_computation.15 | convolution fusion | flops 4838129664 | bytes 20447232 | tf_op jit(solution)/shard_map/dot_general | solution.py:64
  120.9 1.9 copy.32
  122.8 38.0 %all-to-all-done.1 = bf16[4,768,512]{1,2,0:T(8,128)(2,1)} async-done(((bf16[4,768,512]{1,2,0:T(8,128)(2,1)}), bf16[4,768,512]{1,2,0:T(8,128)(2,1)}, u32[]{:S(2)}, u32[]{:S(2)}) %all-to-all-start.1) | async-done | bytes 3145760 | tf_op jit(solution)/shard_map/all_to_all | solution.py:22
  160.8 4.7 %all-to-all-start = ((bf16[4,768,512]{1,2,0:T(8,128)(2,1)}), bf16[4,768,512]{1,2,0:T(8,128)(2,1)}, u32[]{:S(2)}, u32[]{:S(2)}) async-start(bf16[4,768,512]{1,2,0:T(8,128)(2,1)} %bitcast.78), calls=%async_computation | async-start | bytes 6291456 | tf_op jit(solution)/shard_map/all_to_all | solution.py:22
  165.5 11.4 %all_gather.26 = bf16[768,512]{1,0:T(8,128)(2,1)S(1)} all-gather(bf16[768,128]{1,0:T(8,128)(2,1)S(1)} %get-tuple-element.25), channel_id=1, replica_groups=mesh['pole'=4,'row'=2,'col'=4] {'pole'}, dimensions={1}, use_global_device_ids=true | all-gather | bytes 983040 | tf_op jit(solution)/shard_map/all_gather | solution.py:17
  176.9 12.1 %all_gather.25 = bf16[768,512]{1,0:T(8,128)(2,1)S(1)} all-gather(bf16[768,128]{1,0:T(8,128)(2,1)S(1)} %get-tuple-element.24), channel_id=1, replica_groups=mesh['pole'=4,'row'=2,'col'=4] {'pole'}, dimensions={1}, use_global_device_ids=true | all-gather | bytes 983040 | tf_op jit(solution)/shard_map/all_gather | solution.py:16
  189.0 2.3 fusion.37
  191.3 2.3 fusion.39
  193.6 1.6 add_convert_fusion
  195.2 1.6 subtract_convert_fusion.4
  196.9 2.7 convert_reduce_fusion
  199.6 1.0 fusion.73
  200.7 1.0 convolution_add_fusion
  201.8 0.9 fusion.80
  202.6 33.2 %all-to-all-done = bf16[4,768,512]{1,2,0:T(8,128)(2,1)} async-done(((bf16[4,768,512]{1,2,0:T(8,128)(2,1)}), bf16[4,768,512]{1,2,0:T(8,128)(2,1)}, u32[]{:S(2)}, u32[]{:S(2)}) %all-to-all-start) | async-done | bytes 3145760 | tf_op jit(solution)/shard_map/all_to_all | solution.py:22
  235.9 2.6 convert_reduce_fusion.1
  238.4 1.0 fusion.76
  239.5 0.1 copy-done.2
  239.6 1.0 convolution_add_fusion.1
  240.6 0.2 fusion.78
  240.8 0.8 copy-done.8
  241.7 1.3 copy.22
  243.0 29.8 %all_to_all.25 = bf16[8,128,512]{2,1,0:T(8,128)(2,1)S(1)} all-to-all(bf16[8,128,512]{2,1,0:T(8,128)(2,1)} %bitcast.81), channel_id=1, replica_groups=mesh['pole'=4,'row'=2,'col'=4] {'row','col'}, dimensions={0} | all-to-all | bytes 2097152 | tf_op jit(solution)/shard_map/all_to_all | solution.py:22
  272.8 0.8 convert_reduce_fusion.2
  273.6 0.6 fusion.90
  274.2 4.4 %fusion.28 = f32[768,1,512]{0,2,1:T(8,128)} fusion(f32[768,2,256]{0,2,1:T(8,128)} %bitcast.74, f32[768,2,256]{0,2,1:T(8,128)} %bitcast.72, f32[]{:T(128)} %bitcast.18, f32[]{:T(128)} %bitcast.17), kind=kLoop, calls=%fused_computation.41 | loop fusion | flops 1966080 | bytes 4718600 | tf_op jit(solution)/shard_map/sub | solution.py:95
  278.7 3.1 copy.23
  281.8 4.4 %all-to-all-start.3 = ((f32[4,768,128]{2,1,0:T(8,128)}), f32[4,768,128]{2,1,0:T(8,128)}, u32[]{:S(2)}, u32[]{:S(2)}) async-start(f32[4,768,128]{2,1,0:T(8,128)} %copy.23), calls=%async_computation.3 | async-start | bytes 3145728 | tf_op jit(solution)/shard_map/all_to_all | solution.py:22
  286.1 8.5 %all-gather.8.cloned.1.call-done = bf16[1024,512]{1,0:T(8,128)(2,1)} async-done(((bf16[128,512]{1,0:T(8,128)(2,1)}), bf16[1024,512]{1,0:T(8,128)(2,1)}) %all-gather.8.cloned.1.call-update) | async-done | bytes 1048592 | tf_op jit(solution)/shard_map/all_gather | solution.py:92
  294.6 1.5 convert_element_type.115
  296.2 0.5 bitcast_subtract_fusion
  296.7 0.8 copy-done.5
  297.5 2.5 fusion.43
  300.0 6.3 %all-to-all-done.3 = f32[4,768,128]{2,1,0:T(8,128)} async-done(((f32[4,768,128]{2,1,0:T(8,128)}), f32[4,768,128]{2,1,0:T(8,128)}, u32[]{:S(2)}, u32[]{:S(2)}) %all-to-all-start.3) | async-done | bytes 1572896 | tf_op jit(solution)/shard_map/all_to_all | solution.py:22
  306.2 3.5 %all-to-all-start.4 = ((f32[4,128,512]{2,1,0:T(8,128)}), f32[4,128,512]{2,1,0:T(8,128)S(1)}, u32[]{:S(2)}, u32[]{:S(2)}) async-start(f32[4,128,512]{2,1,0:T(8,128)} %bitcast.23), calls=%async_computation.4 | async-start | bytes 2097152 | tf_op jit(solution)/shard_map/all_to_all | solution.py:22
  309.8 3.7 %fusion.19 = f32[1,768,2,512]{1,3,2,0:T(8,128)} fusion(f32[768,2,256]{0,2,1:T(8,128)} %bitcast.73, f32[768,2,256]{0,2,1:T(8,128)} %bitcast.75), kind=kLoop, calls=%fused_computation.22 | loop fusion | flops 786432 | bytes 6291456 | tf_op jit(solution)/shard_map/broadcast_in_dim | solution.py:102
  313.5 5.7 %copy.24 = f32[1,768,2,512]{3,2,1,0:T(2,128)} copy(f32[1,768,2,512]{1,3,2,0:T(8,128)} %fusion.19) | data formatting | bytes 6291456
  319.2 2.3 reduce_sum.48
  321.5 3.4 %sub.62 = f32[1,2,512,512]{3,2,1,0:T(8,128)} subtract(f32[1,2,512,512]{3,2,1,0:T(8,128)S(1)} %copy-done, f32[1,2,512,512]{3,2,1,0:T(8,128)} %bitcast.77) | non-fusion elementwise | flops 524288 | bytes 6291456 | tf_op jit(solution)/shard_map/sub | solution.py:93
  324.9 0.8 reduce_sum.49
  (26 shorter events, 0.4 us)
Async XLA Ops:
  7.2 17.4 %copy-start = (f32[1,2,512,512]{3,2,1,0:T(8,128)S(1)}, f32[1,2,512,512]{3,2,1,0:T(8,128)}, u32[]{:S(2)}) copy-start(f32[1,2,512,512]{3,2,1,0:T(8,128)} %param.10) | copy-start | bytes 6291460
  7.2 58.3 %all-gather.6.cloned.1.call-start = ((), (), s32[]{:S(2)}) async-start(), calls=%async_computation.6 | async-start | bytes 2359296 | tf_op jit(solution)/shard_map/all_gather | solution.py:62
  9.3 2.7 collective-permute-start
  65.5 1.9 copy-start.6
  84.6 76.2 %all-to-all-start.1 = ((bf16[4,768,512]{1,2,0:T(8,128)(2,1)}), bf16[4,768,512]{1,2,0:T(8,128)(2,1)}, u32[]{:S(2)}, u32[]{:S(2)}) async-start(bf16[4,768,512]{1,2,0:T(8,128)(2,1)} %bitcast.79), calls=%async_computation.1 | async-start | bytes 6291456 | tf_op jit(solution)/shard_map/all_to_all | solution.py:22
  89.4 14.2 %all-gather.4.cloned.1.call-start = ((), (), s32[]{:S(2)}) async-start(), calls=%async_computation.5 | async-start | bytes 2359296 | tf_op jit(solution)/shard_map/all_gather | solution.py:62
  103.7 1.9 copy-start.7
  160.8 75.1 %all-to-all-start = ((bf16[4,768,512]{1,2,0:T(8,128)(2,1)}), bf16[4,768,512]{1,2,0:T(8,128)(2,1)}, u32[]{:S(2)}, u32[]{:S(2)}) async-start(bf16[4,768,512]{1,2,0:T(8,128)(2,1)} %bitcast.78), calls=%async_computation | async-start | bytes 6291456 | tf_op jit(solution)/shard_map/all_to_all | solution.py:22
  165.4 129.2 %all-gather.8.cloned.1.call-start = ((), (), s32[]{:S(2)}) async-start(), calls=%async_computation.7 | async-start | bytes 1179648 | tf_op jit(solution)/shard_map/all_gather | solution.py:92
  196.9 3.7 %copy-start.3 = (bf16[768,512]{0,1:T(8,128)(2,1)}, bf16[768,512]{0,1:T(8,128)(2,1)S(1)}, u32[]{:S(2)}) copy-start(bf16[768,512]{0,1:T(8,128)(2,1)S(1)} %subtract_convert_fusion.4) | copy-start | bytes 2359300
  199.6 1.1 copy-start.1
  235.9 2.6 copy-start.4
  238.4 1.2 copy-start.2
  240.6 1.0 copy-start.8
  243.0 30.6 %copy-start.9 = (f32[1,2]{1,0:T(1,128)S(1)}, f32[1,2]{1,0:T(1,128)}, u32[]{:S(2)}) copy-start(f32[1,2]{1,0:T(1,128)} %param.9) | copy-start | bytes 28
  281.8 24.5 %all-to-all-start.3 = ((f32[4,768,128]{2,1,0:T(8,128)}), f32[4,768,128]{2,1,0:T(8,128)}, u32[]{:S(2)}, u32[]{:S(2)}) async-start(f32[4,768,128]{2,1,0:T(8,128)} %copy.23), calls=%async_computation.3 | async-start | bytes 3145728 | tf_op jit(solution)/shard_map/all_to_all | solution.py:22
  296.2 1.3 copy-start.5
  306.2 18.7 %all-to-all-start.4 = ((f32[4,128,512]{2,1,0:T(8,128)}), f32[4,128,512]{2,1,0:T(8,128)S(1)}, u32[]{:S(2)}, u32[]{:S(2)}) async-start(f32[4,128,512]{2,1,0:T(8,128)} %bitcast.23), calls=%async_computation.4 | async-start | bytes 2097152 | tf_op jit(solution)/shard_map/all_to_all | solution.py:22
Sparse Core Ops, SparseCore 0:
  45.8 19.6 all-gather.5
  92.4 11.2 all-gather.3
  273.7 20.8 all-gather.7

commit v3 on v2

--- a/solution.py
+++ b/solution.py
@@ -55,11 +55,13 @@
     met_pair = gather_panel(lax.ppermute(own_pair, ("row", "col"), order))
     met_real, met_imag = factor_panel(met_pair, shift, inverse)
 
+    cuts = [slice(h * part, (h + 1) * part) for h in range(HALVES)]
+    mine = jnp.concatenate([side[:, cut] for cut in cuts for side in (met_real, met_imag)], axis=1)
+    met = lax.all_gather(mine, "row", axis=0, tiled=True)
+
     partials = []
     for h in range(HALVES):
-        cut = slice(h * part, (h + 1) * part)
-        mine = jnp.concatenate([met_real[:, cut], met_imag[:, cut]], axis=1)
-        rows = lax.all_gather(mine, "row", axis=0, tiled=True)
+        rows = met[:, 2 * h * part : 2 * (h + 1) * part]
         turned = jnp.concatenate([rows[:, part:], -rows[:, :part]], axis=1)
         total = jnp.dot(block_imag, turned, preferred_element_type=jnp.float32) - jnp.dot(
             block_real, rows, preferred_element_type=jnp.float32

time: 333 us -> 338 us (1.015)
  waiting for transfers between devices: 119 us -> 124 us
    all_to_all x4, waiting for transfers between devices: 77.5 us -> 93.7 us  [exchange_sum(): lax.all_to_all(pieces, axis, 0, 0, tiled=True).astype(jnp.float32)]
    all_gather x2 -> x1, waiting for transfers between devices: 33.1 us -> 22.2 us  [body(): met = lax.all_gather(mine, 'row', axis=0, tiled=True)]
  transfers between devices with their start and end apart: 8 -> 7, of which waited for: 6 -> 5; matrix products, arithmetic and copies ran while one was open for 19% -> 18% of each run, Pallas kernels for 0% -> 0%
where the time goes in v3:
time: 338 us; the launch traced here: 337 us
  waiting for transfers between devices  124 us (37%)
  blocking collectives  78 us (23%)
  matrix products  50.9 us (15%)
  other arithmetic  30.5 us (9%)
  local copies, waits for them, and re-layouts  19.9 us (6%)
  starting transfers between devices  18.2 us (5%)
  between operations  15 us (4%)
    all_to_all x4, waiting for transfers between devices, exchange_sum(): lax.all_to_all(pieces, axis, 0, 0, tiled=True).astype(jnp.float32)  93.7 us
    all_to_all x1, blocking collectives, exchange_sum(): lax.all_to_all(pieces, axis, 0, 0, tiled=True).astype(jnp.float32)  29.8 us
    all_gather x2, blocking collectives, gather_panel(): lax.all_gather(pair[rows:], 'pole', axis=1, tiled=True)  24.7 us
    all_gather x2, blocking collectives, gather_panel(): lax.all_gather(pair[:rows], 'pole', axis=1, tiled=True)  23.5 us
    all_gather x1, waiting for transfers between devices, body(): met = lax.all_gather(mine, 'row', axis=0, tiled=True)  22.2 us
    all_to_all x4, starting transfers between devices, exchange_sum(): lax.all_to_all(pieces, axis, 0, 0, tiled=True).astype(jnp.float32)  17.4 us
    dot_general x2, matrix products, body(): jnp.dot(block_real, rows, preferred_element_type=jnp.float32)  15.9 us
    dot_general x8, matrix products, precise(): jnp.dot(left, right, precision=lax.Precision.HIGH, preferred_element_type...  15.6 us
  transfers between devices with their start and end apart: 7, of which 5 were waited for; matrix products, arithmetic and copies ran while one was open for 18% of the time, Pallas kernels for 0%

profile of v3, /device:TPU:0, one launch (start us, length us, event | category | flops | bytes accessed | tf_op | source)
XLA Modules:
  0.0 336.6 jit_solution(17290952900891869823)
XLA Ops:
  7.2 0.0 all-gather.3.cloned.1.call-start
  7.2 1.1 constant_dynamic-update-slice_fusion.1
  8.3 1.0 constant_dynamic-update-slice_fusion
  9.3 0.7 collective-permute-start
  10.0 1.3 fusion.92
  12.0 12.6 %all_gather.19 = bf16[768,512]{1,0:T(8,128)(2,1)S(1)} all-gather(bf16[768,128]{1,0:T(8,128)(2,1)S(1)} %get-tuple-element.27), channel_id=1, replica_groups=mesh['pole'=4,'row'=2,'col'=4] {'pole'}, dimensions={1}, use_global_device_ids=true | all-gather | bytes 983040 | tf_op jit(solution)/shard_map/all_gather | solution.py:17
  24.5 1.6 fusion.20
  26.2 1.6 fusion.21
  27.8 12.2 %all_gather.18 = bf16[768,512]{1,0:T(8,128)(2,1)S(1)} all-gather(bf16[768,128]{1,0:T(8,128)(2,1)S(1)} %get-tuple-element.26), channel_id=1, replica_groups=mesh['pole'=4,'row'=2,'col'=4] {'pole'}, dimensions={1}, use_global_device_ids=true | all-gather | bytes 983040 | tf_op jit(solution)/shard_map/all_gather | solution.py:16
  40.0 2.3 add_convert_fusion.1
  42.3 2.3 subtract_convert_fusion.5
  44.6 0.1 fusion.87
  44.7 1.2 pad_maximum_fusion.1
  46.0 0.0 all-gather.3.cloned.1.call-update
  46.0 22.2 %all-gather.3.cloned.1.call-done = bf16[1536,1024]{0,1:T(8,128)(2,1)} async-done(((bf16[768,1024]{0,1:T(8,128)(2,1)}), bf16[1536,1024]{0,1:T(8,128)(2,1)}) %all-gather.3.cloned.1.call-update) | async-done | bytes 3145744 | tf_op jit(solution)/shard_map/all_gather | solution.py:60
  68.2 3.1 fusion.86
  71.2 7.7 %fusion.2 = f32[512,3072]{1,0:T(8,128)S(1)} fusion(bf16[1,2,3072,1536]{3,2,1,0:T(8,128)(2,1)} %param.11, bf16[1536,1024]{0,1:T(8,128)(2,1)S(1)} %copy-done.6), kind=kOutput, calls=%fused_computation.2 | convolution fusion | flops 4831838208 | bytes 17301504 | tf_op jit(solution)/shard_map/dot_general | solution.py:66
  78.9 7.6 %subtract_convert_fusion.1 = bf16[512,3072]{1,0:T(8,128)(2,1)S(1)} fusion(f32[512,3072]{1,0:T(8,128)S(1)} %fusion.2, bf16[1,2,3072,1536]{3,2,1,0:T(8,128)(2,1)} %param.11, bf16[1536,256]{0,1:T(8,128)(2,1)S(1)} %get-tuple-element.15, bf16[1536,256]{0,1:T(8,128)(2,1)S(1)} %get-tuple-element.12), kind=kOutput, calls=%fused_computation.15 | convolution fusion | flops 4838129664 | bytes 20447232 | tf_op jit(solution)/shard_map/dot_general | solution.py:66
  86.6 1.9 copy.32
  88.5 4.9 %all-to-all-start = ((bf16[4,768,512]{1,2,0:T(8,128)(2,1)}), bf16[4,768,512]{1,2,0:T(8,128)(2,1)}, u32[]{:S(2)}, u32[]{:S(2)}) async-start(bf16[4,768,512]{1,2,0:T(8,128)(2,1)} %bitcast.77), calls=%async_computation | async-start | bytes 6291456 | tf_op jit(solution)/shard_map/all_to_all | solution.py:22
  93.3 8.2 %fusion = f32[512,3072]{1,0:T(8,128)S(1)} fusion(bf16[1,2,3072,1536]{3,2,1,0:T(8,128)(2,1)} %param.11, bf16[1536,1024]{0,1:T(8,128)(2,1)} %all-gather.3.cloned.1.call-done), kind=kOutput, calls=%fused_computation | convolution fusion | flops 4831838208 | bytes 17301504 | tf_op jit(solution)/shard_map/dot_general | solution.py:66
  101.5 7.6 %fusion.16 = bf16[3072,512]{0,1:T(8,128)(2,1)S(1)} fusion(f32[512,3072]{1,0:T(8,128)S(1)} %fusion, bf16[1,2,3072,1536]{3,2,1,0:T(8,128)(2,1)} %param.11, bf16[1536,256]{0,1:T(8,128)(2,1)S(1)} %get-tuple-element.13, bf16[1536,256]{0,1:T(8,128)(2,1)S(1)} %copy-done.8), kind=kOutput, calls=%fused_computation.21 | convolution fusion | flops 4838129664 | bytes 20447232 | tf_op jit(solution)/shard_map/dot_general | solution.py:66
  109.2 1.9 copy.31
  111.1 53.7 %all-to-all-done = bf16[4,768,512]{1,2,0:T(8,128)(2,1)} async-done(((bf16[4,768,512]{1,2,0:T(8,128)(2,1)}), bf16[4,768,512]{1,2,0:T(8,128)(2,1)}, u32[]{:S(2)}, u32[]{:S(2)}) %all-to-all-start) | async-done | bytes 3145760 | tf_op jit(solution)/shard_map/all_to_all | solution.py:22
  164.8 4.7 %all-to-all-start.1 = ((bf16[4,768,512]{1,2,0:T(8,128)(2,1)}), bf16[4,768,512]{1,2,0:T(8,128)(2,1)}, u32[]{:S(2)}, u32[]{:S(2)}) async-start(bf16[4,768,512]{1,2,0:T(8,128)(2,1)} %bitcast.76), calls=%async_computation.1 | async-start | bytes 6291456 | tf_op jit(solution)/shard_map/all_to_all | solution.py:22
  169.5 0.0 all-gather.5.cloned.1.call-start
  169.5 11.3 %all_gather.21 = bf16[768,512]{1,0:T(8,128)(2,1)S(1)} all-gather(bf16[768,128]{1,0:T(8,128)(2,1)S(1)} %get-tuple-element.24), channel_id=1, replica_groups=mesh['pole'=4,'row'=2,'col'=4] {'pole'}, dimensions={1}, use_global_device_ids=true | all-gather | bytes 983040 | tf_op jit(solution)/shard_map/all_gather | solution.py:16
  180.8 12.1 %all_gather.22 = bf16[768,512]{1,0:T(8,128)(2,1)S(1)} all-gather(bf16[768,128]{1,0:T(8,128)(2,1)S(1)} %get-tuple-element.25), channel_id=1, replica_groups=mesh['pole'=4,'row'=2,'col'=4] {'pole'}, dimensions={1}, use_global_device_ids=true | all-gather | bytes 983040 | tf_op jit(solution)/shard_map/all_gather | solution.py:17
  192.9 2.3 fusion.41
  195.2 2.3 fusion.39
  197.5 1.6 subtract_convert_fusion.4
  199.1 1.6 add_convert_fusion
  200.8 2.7 convert_reduce_fusion.1
  203.5 1.0 fusion.78
  204.5 0.1 copy-done.1
  204.6 1.0 convolution_add_fusion.1
  205.6 0.9 fusion.80
  206.5 33.6 %all-to-all-done.1 = bf16[4,768,512]{1,2,0:T(8,128)(2,1)} async-done(((bf16[4,768,512]{1,2,0:T(8,128)(2,1)}), bf16[4,768,512]{1,2,0:T(8,128)(2,1)}, u32[]{:S(2)}, u32[]{:S(2)}) %all-to-all-start.1) | async-done | bytes 3145760 | tf_op jit(solution)/shard_map/all_to_all | solution.py:22
  240.1 2.6 convert_reduce_fusion
  242.7 1.0 fusion.75
  243.7 0.1 copy-done.2
  243.8 1.0 convolution_add_fusion
  244.8 0.2 fusion.82
  245.0 0.8 copy-done.7
  245.8 0.1 maximum_maximum_fusion
  245.9 1.3 copy.22
  247.2 29.8 %all_to_all.25 = bf16[8,128,512]{2,1,0:T(8,128)(2,1)S(1)} all-to-all(bf16[8,128,512]{2,1,0:T(8,128)(2,1)} %bitcast.79), channel_id=1, replica_groups=mesh['pole'=4,'row'=2,'col'=4] {'row','col'}, dimensions={0} | all-to-all | bytes 2097152 | tf_op jit(solution)/shard_map/all_to_all | solution.py:22
  277.0 0.8 convert_reduce_fusion.2
  277.8 0.6 fusion.91
  278.4 4.4 %fusion.28 = f32[768,1,512]{0,2,1:T(8,128)} fusion(f32[768,2,256]{0,2,1:T(8,128)} %bitcast.70, f32[768,2,256]{0,2,1:T(8,128)} %bitcast.72, f32[]{:T(128)} %bitcast.18, f32[]{:T(128)} %bitcast.17), kind=kLoop, calls=%fused_computation.41 | loop fusion | flops 1966080 | bytes 4718600 | tf_op jit(solution)/shard_map/sub | solution.py:97
  282.8 3.1 copy.23
  286.0 4.4 %all-to-all-start.3 = ((f32[4,768,128]{2,1,0:T(8,128)}), f32[4,768,128]{2,1,0:T(8,128)}, u32[]{:S(2)}, u32[]{:S(2)}) async-start(f32[4,768,128]{2,1,0:T(8,128)} %copy.23), calls=%async_computation.3 | async-start | bytes 3145728 | tf_op jit(solution)/shard_map/all_to_all | solution.py:22
  290.3 8.2 %all-gather.5.cloned.1.call-done = bf16[1024,512]{1,0:T(8,128)(2,1)} async-done(((bf16[128,512]{1,0:T(8,128)(2,1)}), bf16[1024,512]{1,0:T(8,128)(2,1)}) %all-gather.5.cloned.1.call-update) | async-done | bytes 1048592 | tf_op jit(solution)/shard_map/all_gather | solution.py:94
  298.5 1.5 convert_element_type.115
  300.1 0.5 bitcast_subtract_fusion
  300.5 0.8 copy-done.5
  301.4 2.5 fusion.45
  303.9 6.4 %all-to-all-done.3 = f32[4,768,128]{2,1,0:T(8,128)} async-done(((f32[4,768,128]{2,1,0:T(8,128)}), f32[4,768,128]{2,1,0:T(8,128)}, u32[]{:S(2)}, u32[]{:S(2)}) %all-to-all-start.3) | async-done | bytes 1572896 | tf_op jit(solution)/shard_map/all_to_all | solution.py:22
  310.3 3.5 %all-to-all-start.4 = ((f32[4,128,512]{2,1,0:T(8,128)}), f32[4,128,512]{2,1,0:T(8,128)S(1)}, u32[]{:S(2)}, u32[]{:S(2)}) async-start(f32[4,128,512]{2,1,0:T(8,128)} %bitcast.23), calls=%async_computation.4 | async-start | bytes 2097152 | tf_op jit(solution)/shard_map/all_to_all | solution.py:22
  313.8 3.7 %fusion.19 = f32[1,768,2,512]{1,3,2,0:T(8,128)} fusion(f32[768,2,256]{0,2,1:T(8,128)} %bitcast.73, f32[768,2,256]{0,2,1:T(8,128)} %bitcast.71), kind=kLoop, calls=%fused_computation.22 | loop fusion | flops 786432 | bytes 6291456 | tf_op jit(solution)/shard_map/broadcast_in_dim | solution.py:104
  317.5 5.7 %copy.24 = f32[1,768,2,512]{3,2,1,0:T(2,128)} copy(f32[1,768,2,512]{1,3,2,0:T(8,128)} %fusion.19) | data formatting | bytes 6291456
  323.3 2.3 reduce_sum.48
  325.5 3.4 %sub.62 = f32[1,2,512,512]{3,2,1,0:T(8,128)} subtract(f32[1,2,512,512]{3,2,1,0:T(8,128)S(1)} %copy-done, f32[1,2,512,512]{3,2,1,0:T(8,128)} %bitcast.75) | non-fusion elementwise | flops 524288 | bytes 6291456 | tf_op jit(solution)/shard_map/sub | solution.py:95
  328.9 0.8 reduce_sum.49
  (21 shorter events, 0.1 us)
Async XLA Ops:
  7.2 17.4 %copy-start = (f32[1,2,512,512]{3,2,1,0:T(8,128)S(1)}, f32[1,2,512,512]{3,2,1,0:T(8,128)}, u32[]{:S(2)}) copy-start(f32[1,2,512,512]{3,2,1,0:T(8,128)} %param.10) | copy-start | bytes 6291460
  7.2 61.0 %all-gather.3.cloned.1.call-start = ((), (), s32[]{:S(2)}) async-start(), calls=%async_computation.5 | async-start | bytes 4718592 | tf_op jit(solution)/shard_map/all_gather | solution.py:60
  9.3 2.7 collective-permute-start
  68.2 3.1 copy-start.6
  88.5 76.3 %all-to-all-start = ((bf16[4,768,512]{1,2,0:T(8,128)(2,1)}), bf16[4,768,512]{1,2,0:T(8,128)(2,1)}, u32[]{:S(2)}, u32[]{:S(2)}) async-start(bf16[4,768,512]{1,2,0:T(8,128)(2,1)} %bitcast.77), calls=%async_computation | async-start | bytes 6291456 | tf_op jit(solution)/shard_map/all_to_all | solution.py:22
  93.3 8.2 %copy-start.8 = (bf16[1536,256]{0,1:T(8,128)(2,1)S(1)}, bf16[1536,256]{0,1:T(8,128)(2,1)}, u32[]{:S(2)}) copy-start(bf16[1536,256]{0,1:T(8,128)(2,1)} %get-tuple-element.14) | copy-start | bytes 2359300
  164.8 75.3 %all-to-all-start.1 = ((bf16[4,768,512]{1,2,0:T(8,128)(2,1)}), bf16[4,768,512]{1,2,0:T(8,128)(2,1)}, u32[]{:S(2)}, u32[]{:S(2)}) async-start(bf16[4,768,512]{1,2,0:T(8,128)(2,1)} %bitcast.76), calls=%async_computation.1 | async-start | bytes 6291456 | tf_op jit(solution)/shard_map/all_to_all | solution.py:22
  169.5 129.1 %all-gather.5.cloned.1.call-start = ((), (), s32[]{:S(2)}) async-start(), calls=%async_computation.6 | async-start | bytes 1179648 | tf_op jit(solution)/shard_map/all_gather | solution.py:94
  200.7 3.7 %copy-start.3 = (bf16[768,512]{0,1:T(8,128)(2,1)}, bf16[768,512]{0,1:T(8,128)(2,1)S(1)}, u32[]{:S(2)}) copy-start(bf16[768,512]{0,1:T(8,128)(2,1)S(1)} %add_convert_fusion) | copy-start | bytes 2359300
  203.5 1.2 copy-start.1
  240.1 2.6 copy-start.4
  242.7 1.1 copy-start.2
  244.8 1.0 copy-start.7
  247.2 30.6 %copy-start.9 = (f32[1,2]{1,0:T(1,128)S(1)}, f32[1,2]{1,0:T(1,128)}, u32[]{:S(2)}) copy-start(f32[1,2]{1,0:T(1,128)} %param.9) | copy-start | bytes 28
  286.0 24.3 %all-to-all-start.3 = ((f32[4,768,128]{2,1,0:T(8,128)}), f32[4,768,128]{2,1,0:T(8,128)}, u32[]{:S(2)}, u32[]{:S(2)}) async-start(f32[4,768,128]{2,1,0:T(8,128)} %copy.23), calls=%async_computation.3 | async-start | bytes 3145728 | tf_op jit(solution)/shard_map/all_to_all | solution.py:22
  300.0 1.3 copy-start.5
  310.3 18.7 %all-to-all-start.4 = ((f32[4,128,512]{2,1,0:T(8,128)}), f32[4,128,512]{2,1,0:T(8,128)S(1)}, u32[]{:S(2)}, u32[]{:S(2)}) async-start(f32[4,128,512]{2,1,0:T(8,128)} %bitcast.23), calls=%async_computation.4 | async-start | bytes 2097152 | tf_op jit(solution)/shard_map/all_to_all | solution.py:22
Sparse Core Ops, SparseCore 0:
  46.1 21.9 all-gather.2
  278.0 20.5 all-gather.4
